TPU v7x, 256 devices: a whole 4x4x8 slice. The times are simulated.
256 devices in a mesh: dp: 16 (over z, core), tensor: 16 (over y, x).
Axes of the slice: x: 4, y: 4, z: 8, core: 2. Of those that a mesh axis runs over, the one named last changes fastest.
Arguments:
- activations: bfloat16 [36864, 8192], P('dp', 'tensor'), may hold values from -6 to 6
- out_grads: bfloat16 [36864, 28672], P('dp', 'tensor'), may hold values from -0.0546875 to 0.0546875
- basis: bfloat16 [8192, 256], P('tensor'), may hold values from -0.375 to 0.375
- first_moment: float32 [256, 28672], P('dp', 'tensor'), may hold values from -6 to 6
- second_moment: float32 [256, 28672], P('dp', 'tensor'), may hold values from 0.05 to 0.8
- reward_codes: int32 [36864], P('dp'), may hold values from 0 to 15
- token_ids: int32 [36864], P('dp'), may hold values from 0 to 128004, as said below
Outputs:
- new_first: float32 [256, 28672], P('dp', 'tensor')
- new_second: float32 [256, 28672], P('dp', 'tensor')
- weight_update: bfloat16 [8192, 28672], P('dp', 'tensor')
Inputs may be any that keep to these rules, and one draw needn't show every extreme that they name: `token_ids`: the id 128004 is the padding token; the first of each 2304 consecutive tokens is never padding.
All inputs are finite; a program needn't handle non-finite values.
Results may differ from a plain program's by a relative error of at most 0.019.
Values may be sent and summed in bfloat16 or wider, within the bound.
A program may use at most 64 MiB of HBM per device.

v0:
```python
import jax
import jax.numpy as jnp
from jax import lax
from jax.sharding import PartitionSpec as P

ADAM_STEP = 100
pad_token = 128004
reward_temp = 0.2
beta_one = 0.9
beta_two = 0.999
adam_eps = 1e-08


def filled_up(lines, size):
    spare = -len(lines) % size
    return jnp.pad(lines, [(0, spare)] + [(0, 0)] * (lines.ndim - 1))


def joined_along(parts, dim):
    parts = jnp.moveaxis(parts, 0, dim)
    lengths = parts.shape
    return parts.reshape(*lengths[:dim], lengths[dim] * lengths[dim + 1], *lengths[dim + 2 :])


def sent_to_all(shard, axis):
    size = lax.axis_size(axis)
    return lax.all_to_all(
        jnp.broadcast_to(shard[None], (size, *shard.shape)), axis, 0, 0, tiled=True
    )


def gather_directly(shard, axis, dim):
    return joined_along(sent_to_all(shard, axis), dim)


def split_up(shard, dim, size):
    before, after = (shard.shape[:dim], shard.shape[dim + 1 :])
    return jnp.moveaxis(shard.reshape(*before, size, -1, *after), dim, 0)


def sum_at_owner(shard, axis, dim):
    parts = split_up(shard, dim, lax.axis_size(axis))
    arrived = lax.all_to_all(parts, axis, split_axis=0, concat_axis=0, tiled=True)
    return arrived.astype(jnp.float32).sum(axis=0)


def total_of(shard, axes):
    lines = shard.reshape(-1, shard.shape[-1])
    padded = filled_up(lines, lax.axis_size(axes))
    whole = gather_directly(sum_at_owner(padded, axes, 0).astype(jnp.bfloat16), axes, 0)
    return lax.slice_in_dim(whole, 0, len(lines)).reshape(shard.shape).astype(jnp.float32)


def of_everyone(shard, axis):
    return sent_to_all(shard, axis).sum(axis=0)


def broadcast(shard, axis, root):
    return lax.dynamic_index_in_dim(lax.all_gather(shard, axis), root, 0, keepdims=False)


def local(activations, out_grads, basis, first_moment, second_moment, reward_codes, token_ids):
    data_count = lax.axis_size("dp")
    tensor_count = lax.axis_size("tensor")
    partial_value = jnp.dot(activations, basis, preferred_element_type=jnp.float32)
    projected = total_of(partial_value.astype(jnp.bfloat16), "tensor")
    unmasked = (token_ids != pad_token).astype(jnp.float32)
    weights = unmasked * jnp.exp(reward_temp * reward_codes.astype(jnp.float32))
    local_total = jnp.sum(weights)
    weighted = (weights[:, None] * projected).astype(jnp.bfloat16)
    raw_grad = lax.dot_general(
        weighted, out_grads, (((0,), (0,)), ((), ())), preferred_element_type=jnp.float32
    )
    normalizer = of_everyone(local_total, "dp")
    grad_rows = sum_at_owner(raw_grad.astype(jnp.bfloat16), "dp", 0)
    token_count = activations.shape[0] * data_count
    gradient = grad_rows * (token_count / normalizer)
    new_first = beta_one * first_moment + (1.0 - beta_one) * gradient
    new_second = beta_two * second_moment + (1.0 - beta_two) * gradient * gradient
    bias_one = 1.0 - beta_one**ADAM_STEP
    bias_two = 1.0 - beta_two**ADAM_STEP
    update = (new_first / bias_one / (jnp.sqrt(new_second / bias_two) + adam_eps)).astype(
        jnp.bfloat16
    )
    data_index = lax.axis_index("dp")
    owner_index = data_index * tensor_count // data_count
    owner_rows = broadcast(basis, "tensor", owner_index)
    summed = jnp.dot(
        owner_rows,
        lax.all_gather(update, "dp", axis=0, tiled=True),
        preferred_element_type=jnp.float32,
    )
    return (new_first, new_second, summed.astype(jnp.bfloat16))


def solution(mesh):
    return jax.shard_map(
        local,
        mesh=mesh,
        in_specs=(
            P("dp", "tensor"),
            P("dp", "tensor"),
            P("tensor", None),
            P("dp", "tensor"),
            P("dp", "tensor"),
            P("dp"),
            P("dp"),
        ),
        out_specs=(P("dp", "tensor"), P("dp", "tensor"), P("dp", "tensor")),
        check_vma=False,
    )
```

profile of v0, /device:TPU:1, one launch (start us, length us, event | category | flops | bytes accessed | tf_op | source)
XLA Modules:
  0.0 148.8 jit_solution(3367582259047807124)
XLA Ops:
  7.2 0.0 copy-start
  7.2 0.0 all-gather.3.cloned.1.call-start
  7.2 0.7 all-gather.3.cloned.1.call-update
  7.9 0.9 copy-done
  8.8 1.7 %convolution_convert_fusion = bf16[2304,256]{1,0:T(8,128)(2,1)S(1)} fusion(bf16[2304,512]{1,0:T(8,128)(2,1)S(1)} %copy-done, bf16[512,256]{1,0:T(8,128)(2,1)} %param.9), kind=kOutput, calls=%fused_computation | convolution fusion | flops 604569600 | bytes 3801088 | tf_op jit(solution)/shard_map/dot_general | solution.py:65
  10.6 26.5 %all_to_all.21 = bf16[16,144,256]{2,1,0:T(8,128)(2,1)S(1)} all-to-all(bf16[16,144,256]{2,1,0:T(8,128)(2,1)S(1)} %bitcast.14), channel_id=1, replica_groups=mesh['dp'=16,'tensor'=16] {'tensor'}, dimensions={0} | all-to-all | bytes 2359296 | tf_op jit(solution)/shard_map/all_to_all | solution.py:43
  37.1 0.8 reduce_sum.39
  37.9 2.0 %broadcast_in_dim.4 = bf16[16,144,256]{2,1,0:T(8,128)(2,1)} broadcast(bf16[144,256]{1,0:T(8,128)(2,1)} %reduce_sum.39), dimensions={1,2} | broadcast | bytes 1253376 | tf_op jit(solution)/shard_map/broadcast_in_dim | solution.py:28
  39.9 3.7 %all-to-all-start.1 = ((bf16[16,144,256]{2,1,0:T(8,128)(2,1)}), bf16[16,144,256]{2,1,0:T(8,128)(2,1)S(1)}, u32[]{:S(2)}, u32[]{:S(2)}) async-start(bf16[16,144,256]{2,1,0:T(8,128)(2,1)} %broadcast_in_dim.4), calls=%async_computation.1 | async-start | bytes 2359296 | tf_op jit(solution)/shard_map/all_to_all | solution.py:27
  43.6 1.3 fusion.8
  44.9 14.6 %all-to-all-done.1 = bf16[16,144,256]{2,1,0:T(8,128)(2,1)S(1)} async-done(((bf16[16,144,256]{2,1,0:T(8,128)(2,1)}), bf16[16,144,256]{2,1,0:T(8,128)(2,1)S(1)}, u32[]{:S(2)}, u32[]{:S(2)}) %all-to-all-start.1) | async-done | bytes 1179680 | tf_op jit(solution)/shard_map/all_to_all | solution.py:27
  59.6 1.2 broadcast_in_dim.5
  60.8 21.0 %all-to-all-start.3 = ((f32[16,1,1]{2,1,0:T(1,128)}), f32[16,1,1]{2,1,0:T(1,128)}, u32[]{:S(2)}, u32[]{:S(2)}) async-start(f32[16,1,1]{2,1,0:T(1,128)} %broadcast_in_dim.5), calls=%async_computation.3 | async-start | bytes 16384 | tf_op jit(solution)/shard_map/all_to_all | solution.py:27
  81.9 6.7 %convolution_convert_fusion.2 = bf16[256,1792]{1,0:T(8,128)(2,1)} fusion(bf16[2304,1792]{1,0:T(8,128)(2,1)} %param.8, bf16[2304,256]{1,0:T(8,128)(2,1)S(1)} %bitcast.12, f32[2304]{0:T(1024)S(1)} %get-tuple-element.7), kind=kOutput, calls=%fused_computation.2 | convolution fusion | flops 2116157440 | bytes 10363904 | tf_op jit(solution)/shard_map/dot_general | solution.py:71
  88.6 0.3 all-to-all-done.3
  88.9 7.0 %all-to-all-start.2 = ((bf16[16,16,1792]{2,1,0:T(8,128)(2,1)}), bf16[16,16,1792]{2,1,0:T(8,128)(2,1)S(1)}, u32[]{:S(2)}, u32[]{:S(2)}) async-start(bf16[16,16,1792]{2,1,0:T(8,128)(2,1)} %bitcast.13), calls=%async_computation.2 | async-start | bytes 1835008 | tf_op jit(solution)/shard_map/all_to_all | solution.py:43
  96.0 1.3 reduce_sum.42
  98.0 23.3 %all-to-all-done.2 = bf16[16,16,1792]{2,1,0:T(8,128)(2,1)S(1)} async-done(((bf16[16,16,1792]{2,1,0:T(8,128)(2,1)}), bf16[16,16,1792]{2,1,0:T(8,128)(2,1)S(1)}, u32[]{:S(2)}, u32[]{:S(2)}) %all-to-all-start.2) | async-done | bytes 917536 | tf_op jit(solution)/shard_map/all_to_all | solution.py:43
  121.2 0.1 convert_reduce_fusion
  121.4 0.0 copy-done.1
  121.4 0.0 copy-done.2
  121.4 0.8 divide_convert_fusion
  122.2 17.0 %all_gather.11 = bf16[256,1792]{1,0:T(8,128)(2,1)S(1)} all-gather(bf16[16,1792]{1,0:T(8,128)(2,1)S(1)} %get-tuple-element.3), channel_id=1, replica_groups=mesh['dp'=16,'tensor'=16] {'dp'}, dimensions={0}, use_global_device_ids=true | all-gather | bytes 974848 | tf_op jit(solution)/shard_map/all_gather | solution.py:90
  139.1 2.8 %convolution_convert_fusion.1 = bf16[512,1792]{1,0:T(8,128)(2,1)} fusion(bf16[256,1792]{1,0:T(8,128)(2,1)S(1)} %all_gather.11, bf16[16,512,256]{2,1,0:T(8,128)(2,1)} %bitcast.15, s32[]{:T(128)S(6)} %select_n.10), kind=kOutput, calls=%fused_computation.1 | convolution fusion | flops 470679552 | bytes 3014660 | tf_op jit(solution)/shard_map/dot_general | solution.py:88
  (3 shorter events, 0.0 us)
Async XLA Ops:
  7.2 1.7 %copy-start = (bf16[2304,512]{1,0:T(8,128)(2,1)S(1)}, bf16[2304,512]{1,0:T(8,128)(2,1)}, u32[]{:S(2)}) copy-start(bf16[2304,512]{1,0:T(8,128)(2,1)} %param.7) | copy-start | bytes 7077892
  7.2 132.0 %all-gather.3.cloned.1.call-start = ((), (), s32[]{:S(2)}) async-start(), calls=%async_computation.4 | async-start | bytes 4456448 | tf_op jit(solution)/shard_map/all_gather | solution.py:59
  39.9 19.7 %all-to-all-start.1 = ((bf16[16,144,256]{2,1,0:T(8,128)(2,1)}), bf16[16,144,256]{2,1,0:T(8,128)(2,1)S(1)}, u32[]{:S(2)}, u32[]{:S(2)}) async-start(bf16[16,144,256]{2,1,0:T(8,128)(2,1)} %broadcast_in_dim.4), calls=%async_computation.1 | async-start | bytes 2359296 | tf_op jit(solution)/shard_map/all_to_all | solution.py:27
  60.8 28.1 %all-to-all-start.3 = ((f32[16,1,1]{2,1,0:T(1,128)}), f32[16,1,1]{2,1,0:T(1,128)}, u32[]{:S(2)}, u32[]{:S(2)}) async-start(f32[16,1,1]{2,1,0:T(1,128)} %broadcast_in_dim.5), calls=%async_computation.3 | async-start | bytes 16384 | tf_op jit(solution)/shard_map/all_to_all | solution.py:27
  88.6 32.8 %copy-start.1 = (f32[16,1792]{1,0:T(8,128)S(1)}, f32[16,1792]{1,0:T(8,128)}, u32[]{:S(2)}) copy-start(f32[16,1792]{1,0:T(8,128)} %param.11) | copy-start | bytes 344068
  88.6 32.8 %copy-start.2 = (f32[16,1792]{1,0:T(8,128)S(1)}, f32[16,1792]{1,0:T(8,128)}, u32[]{:S(2)}) copy-start(f32[16,1792]{1,0:T(8,128)} %param.10) | copy-start | bytes 344068
  88.9 32.3 %all-to-all-start.2 = ((bf16[16,16,1792]{2,1,0:T(8,128)(2,1)}), bf16[16,16,1792]{2,1,0:T(8,128)(2,1)S(1)}, u32[]{:S(2)}, u32[]{:S(2)}) async-start(bf16[16,16,1792]{2,1,0:T(8,128)(2,1)} %bitcast.13), calls=%async_computation.2 | async-start | bytes 1835008 | tf_op jit(solution)/shard_map/all_to_all | solution.py:43
Sparse Core Ops, SparseCore 0:
  10.4 67.8 all-gather.2
where the time goes:
time: 149 us
  blocking collectives  43.5 us (29%)
  waiting for transfers between devices  38.9 us (26%)
  starting transfers between devices  31.8 us (21%)
  between operations  14.8 us (10%)
  matrix products  11.3 us (8%)
  other arithmetic  4.34 us (3%)
  local copies, waits for them, and re-layouts  4.16 us (3%)
    all_to_all x1, blocking collectives, sum_at_owner(): lax.all_to_all(parts, axis, split_axis=0, concat_axis=0, tiled=True)  26.5 us
    all_to_all x2, starting transfers between devices, sent_to_all(): lax.all_to_all(jnp.broadcast_to(shard[None], (size, *shard.shape)), axis,...  24.7 us
    all_to_all x1, waiting for transfers between devices, sum_at_owner(): lax.all_to_all(parts, axis, split_axis=0, concat_axis=0, tiled=True)  23.3 us
    all_gather x1, blocking collectives, local(): lax.all_gather(update, 'dp', axis=0, tiled=True)  17 us
    all_to_all x2, waiting for transfers between devices, sent_to_all(): lax.all_to_all(jnp.broadcast_to(shard[None], (size, *shard.shape)), axis,...  15 us
    all_to_all x1, starting transfers between devices, sum_at_owner(): lax.all_to_all(parts, axis, split_axis=0, concat_axis=0, tiled=True)  7.04 us
    dot_general x1, matrix products, local(): lax.dot_general(weighted, out_grads, (((0,), (0,)), ((), ())), preferred_...  6.72 us
    broadcast_in_dim x2, local copies, waits for them, and re-layouts, sent_to_all(): jnp.broadcast_to(shard[None], (size, *shard.shape))  3.22 us
  transfers between devices with their start and end apart: 4, of which 3 were waited for; matrix products, arithmetic and copies ran while one was open for 11% of the time, Pallas kernels for 0%

commit v1 on v0

--- a/solution.py
+++ b/solution.py
@@ -9,6 +9,13 @@
 beta_one = 0.9
 beta_two = 0.999
 adam_eps = 1e-08
+
+
+def swapped_in(shard, axis, d):
+    size = lax.axis_size(axis)
+    pieces = jnp.stack([shard for _ in range(size)])
+    pieces = lax.all_to_all(pieces, axis, split_axis=0, concat_axis=0)
+    return jnp.concatenate(pieces, axis=d)
 
 
 def filled_up(lines, size):
@@ -85,11 +92,7 @@
     data_index = lax.axis_index("dp")
     owner_index = data_index * tensor_count // data_count
     owner_rows = broadcast(basis, "tensor", owner_index)
-    summed = jnp.dot(
-        owner_rows,
-        lax.all_gather(update, "dp", axis=0, tiled=True),
-        preferred_element_type=jnp.float32,
-    )
+    summed = jnp.dot(owner_rows, swapped_in(update, "dp", 0), preferred_element_type=jnp.float32)
     return (new_first, new_second, summed.astype(jnp.bfloat16))
 
 

time: 149 us -> 162 us (1.087)
  waiting for transfers between devices: 38.9 us -> 63.9 us
  blocking collectives: 43.5 us -> 26.5 us
  starting transfers between devices: 31.8 us -> 35.5 us
    all_to_all x0 -> x1, waiting for transfers between devices: none -> 25.1 us  [swapped_in(): pieces = lax.all_to_all(pieces, axis, split_axis=0, concat_axis=0)]
    all_gather x1 -> x0, blocking collectives: 17 us -> none  [local(): lax.all_gather(update, 'dp', axis=0, tiled=True)]
    all_to_all x0 -> x1, starting transfers between devices: none -> 3.53 us  [swapped_in(): pieces = lax.all_to_all(pieces, axis, split_axis=0, concat_axis=0)]
  transfers between devices with their start and end apart: 4 -> 5, of which waited for: 3 -> 4; matrix products, arithmetic and copies ran while one was open for 11% -> 11% of each run, Pallas kernels for 0% -> 0%
where the time goes in v1:
time: 162 us; the launch traced here: 161 us
  waiting for transfers between devices  63.9 us (39%)
  starting transfers between devices  35.5 us (22%)
  blocking collectives  26.5 us (16%)
  between operations  14.8 us (9%)
  matrix products  11.3 us (7%)
  local copies, waits for them, and re-layouts  5.14 us (3%)
  other arithmetic  4.34 us (3%)
    all_to_all x1, blocking collectives, sum_at_owner(): lax.all_to_all(parts, axis, split_axis=0, concat_axis=0, tiled=True)  26.5 us
    all_to_all x1, waiting for transfers between devices, swapped_in(): pieces = lax.all_to_all(pieces, axis, split_axis=0, concat_axis=0)  25.1 us
    all_to_all x2, starting transfers between devices, sent_to_all(): lax.all_to_all(jnp.broadcast_to(shard[None], (size, *shard.shape)), axis,...  24.7 us
    all_to_all x1, waiting for transfers between devices, sum_at_owner(): lax.all_to_all(parts, axis, split_axis=0, concat_axis=0, tiled=True)  23.3 us
    all_to_all x2, waiting for transfers between devices, sent_to_all(): lax.all_to_all(jnp.broadcast_to(shard[None], (size, *shard.shape)), axis,...  14.8 us
    all_to_all x1, starting transfers between devices, sum_at_owner(): lax.all_to_all(parts, axis, split_axis=0, concat_axis=0, tiled=True)  7.19 us
    dot_general x1, matrix products, local(): lax.dot_general(weighted, out_grads, (((0,), (0,)), ((), ())), preferred_...  6.72 us
    all_to_all x1, starting transfers between devices, swapped_in(): pieces = lax.all_to_all(pieces, axis, split_axis=0, concat_axis=0)  3.53 us
  transfers between devices with their start and end apart: 5, of which 4 were waited for; matrix products, arithmetic and copies ran while one was open for 11% of the time, Pallas kernels for 0%

profile of v1, /device:TPU:1, one launch (start us, length us, event | category | flops | bytes accessed | tf_op | source)
XLA Modules:
  0.0 161.5 jit_solution(4987566184697905584)
XLA Ops:
  7.2 0.0 copy-start
  7.2 0.0 all-gather.3.cloned.1.call-start
  7.2 0.7 all-gather.3.cloned.1.call-update
  7.9 0.9 copy-done
  8.8 1.7 %convolution_convert_fusion = bf16[2304,256]{1,0:T(8,128)(2,1)S(1)} fusion(bf16[2304,512]{1,0:T(8,128)(2,1)S(1)} %copy-done, bf16[512,256]{1,0:T(8,128)(2,1)} %param.9), kind=kOutput, calls=%fused_computation | convolution fusion | flops 604569600 | bytes 3801088 | tf_op jit(solution)/shard_map/dot_general | solution.py:72
  10.6 26.5 %all_to_all.26 = bf16[16,144,256]{2,1,0:T(8,128)(2,1)S(1)} all-to-all(bf16[16,144,256]{2,1,0:T(8,128)(2,1)S(1)} %bitcast.16), channel_id=1, replica_groups=mesh['dp'=16,'tensor'=16] {'tensor'}, dimensions={0} | all-to-all | bytes 2359296 | tf_op jit(solution)/shard_map/all_to_all | solution.py:50
  37.1 0.8 reduce_sum.39
  37.9 2.0 %broadcast_in_dim.4 = bf16[16,144,256]{2,1,0:T(8,128)(2,1)} broadcast(bf16[144,256]{1,0:T(8,128)(2,1)} %reduce_sum.39), dimensions={1,2} | broadcast | bytes 1253376 | tf_op jit(solution)/shard_map/broadcast_in_dim | solution.py:35
  39.9 3.7 %all-to-all-start.1 = ((bf16[16,144,256]{2,1,0:T(8,128)(2,1)}), bf16[16,144,256]{2,1,0:T(8,128)(2,1)S(1)}, u32[]{:S(2)}, u32[]{:S(2)}) async-start(bf16[16,144,256]{2,1,0:T(8,128)(2,1)} %broadcast_in_dim.4), calls=%async_computation.1 | async-start | bytes 2359296 | tf_op jit(solution)/shard_map/all_to_all | solution.py:34
  43.6 1.3 fusion.8
  44.9 14.6 %all-to-all-done.1 = bf16[16,144,256]{2,1,0:T(8,128)(2,1)S(1)} async-done(((bf16[16,144,256]{2,1,0:T(8,128)(2,1)}), bf16[16,144,256]{2,1,0:T(8,128)(2,1)S(1)}, u32[]{:S(2)}, u32[]{:S(2)}) %all-to-all-start.1) | async-done | bytes 1179680 | tf_op jit(solution)/shard_map/all_to_all | solution.py:34
  59.6 1.2 broadcast_in_dim.5
  60.8 21.0 %all-to-all-start.3 = ((f32[16,1,1]{2,1,0:T(1,128)}), f32[16,1,1]{2,1,0:T(1,128)}, u32[]{:S(2)}, u32[]{:S(2)}) async-start(f32[16,1,1]{2,1,0:T(1,128)} %broadcast_in_dim.5), calls=%async_computation.3 | async-start | bytes 16384 | tf_op jit(solution)/shard_map/all_to_all | solution.py:34
  81.9 6.7 %convolution_convert_fusion.2 = bf16[256,1792]{1,0:T(8,128)(2,1)} fusion(bf16[2304,1792]{1,0:T(8,128)(2,1)} %param.8, bf16[2304,256]{1,0:T(8,128)(2,1)S(1)} %bitcast.13, f32[2304]{0:T(1024)S(1)} %get-tuple-element.7), kind=kOutput, calls=%fused_computation.2 | convolution fusion | flops 2116157440 | bytes 10363904 | tf_op jit(solution)/shard_map/dot_general | solution.py:78
  88.6 0.2 all-to-all-done.3
  88.8 7.2 %all-to-all-start.2 = ((bf16[16,16,1792]{2,1,0:T(8,128)(2,1)}), bf16[16,16,1792]{2,1,0:T(8,128)(2,1)S(1)}, u32[]{:S(2)}, u32[]{:S(2)}) async-start(bf16[16,16,1792]{2,1,0:T(8,128)(2,1)} %bitcast.15), calls=%async_computation.2 | async-start | bytes 1835008 | tf_op jit(solution)/shard_map/all_to_all | solution.py:50
  96.0 1.3 reduce_sum.42
  98.0 23.3 %all-to-all-done.2 = bf16[16,16,1792]{2,1,0:T(8,128)(2,1)S(1)} async-done(((bf16[16,16,1792]{2,1,0:T(8,128)(2,1)}), bf16[16,16,1792]{2,1,0:T(8,128)(2,1)S(1)}, u32[]{:S(2)}, u32[]{:S(2)}) %all-to-all-start.2) | async-done | bytes 917536 | tf_op jit(solution)/shard_map/all_to_all | solution.py:50
  121.2 0.1 convert_reduce_fusion
  121.4 0.8 divide_convert_fusion
  122.2 1.0 stack.2
  123.1 3.5 %all-to-all-start.4 = ((bf16[16,16,1792]{2,1,0:T(8,128)(2,1)}), bf16[16,16,1792]{2,1,0:T(8,128)(2,1)S(1)}, u32[]{:S(2)}, u32[]{:S(2)}) async-start(bf16[16,16,1792]{2,1,0:T(8,128)(2,1)} %stack.2), calls=%async_computation.4 | async-start | bytes 1835008 | tf_op jit(solution)/shard_map/all_to_all | solution.py:17
  126.7 25.1 %all-to-all-done.4 = bf16[16,16,1792]{2,1,0:T(8,128)(2,1)S(1)} async-done(((bf16[16,16,1792]{2,1,0:T(8,128)(2,1)}), bf16[16,16,1792]{2,1,0:T(8,128)(2,1)S(1)}, u32[]{:S(2)}, u32[]{:S(2)}) %all-to-all-start.4) | async-done | bytes 917536 | tf_op jit(solution)/shard_map/all_to_all | solution.py:17
  151.8 2.8 %convolution_convert_fusion.1 = bf16[512,1792]{1,0:T(8,128)(2,1)} fusion(bf16[256,1792]{1,0:T(8,128)(2,1)S(1)} %bitcast.14, bf16[16,512,256]{2,1,0:T(8,128)(2,1)} %bitcast.17, s32[]{:T(128)S(6)} %select_n.10), kind=kOutput, calls=%fused_computation.1 | convolution fusion | flops 470679552 | bytes 3014660 | tf_op jit(solution)/shard_map/dot_general | solution.py:95
  (5 shorter events, 0.0 us)
Async XLA Ops:
  7.2 1.7 %copy-start = (bf16[2304,512]{1,0:T(8,128)(2,1)S(1)}, bf16[2304,512]{1,0:T(8,128)(2,1)}, u32[]{:S(2)}) copy-start(bf16[2304,512]{1,0:T(8,128)(2,1)} %param.7) | copy-start | bytes 7077892
  7.2 144.6 %all-gather.3.cloned.1.call-start = ((), (), s32[]{:S(2)}) async-start(), calls=%async_computation.5 | async-start | bytes 4456448 | tf_op jit(solution)/shard_map/all_gather | solution.py:66
  39.9 19.7 %all-to-all-start.1 = ((bf16[16,144,256]{2,1,0:T(8,128)(2,1)}), bf16[16,144,256]{2,1,0:T(8,128)(2,1)S(1)}, u32[]{:S(2)}, u32[]{:S(2)}) async-start(bf16[16,144,256]{2,1,0:T(8,128)(2,1)} %broadcast_in_dim.4), calls=%async_computation.1 | async-start | bytes 2359296 | tf_op jit(solution)/shard_map/all_to_all | solution.py:34
  60.8 27.9 %all-to-all-start.3 = ((f32[16,1,1]{2,1,0:T(1,128)}), f32[16,1,1]{2,1,0:T(1,128)}, u32[]{:S(2)}, u32[]{:S(2)}) async-start(f32[16,1,1]{2,1,0:T(1,128)} %broadcast_in_dim.5), calls=%async_computation.3 | async-start | bytes 16384 | tf_op jit(solution)/shard_map/all_to_all | solution.py:34
  88.6 32.8 %copy-start.1 = (f32[16,1792]{1,0:T(8,128)S(1)}, f32[16,1792]{1,0:T(8,128)}, u32[]{:S(2)}) copy-start(f32[16,1792]{1,0:T(8,128)} %param.11) | copy-start | bytes 344068
  88.6 32.8 %copy-start.2 = (f32[16,1792]{1,0:T(8,128)S(1)}, f32[16,1792]{1,0:T(8,128)}, u32[]{:S(2)}) copy-start(f32[16,1792]{1,0:T(8,128)} %param.10) | copy-start | bytes 344068
  88.8 32.5 %all-to-all-start.2 = ((bf16[16,16,1792]{2,1,0:T(8,128)(2,1)}), bf16[16,16,1792]{2,1,0:T(8,128)(2,1)S(1)}, u32[]{:S(2)}, u32[]{:S(2)}) async-start(bf16[16,16,1792]{2,1,0:T(8,128)(2,1)} %bitcast.15), calls=%async_computation.2 | async-start | bytes 1835008 | tf_op jit(solution)/shard_map/all_to_all | solution.py:50
  123.1 28.6 %all-to-all-start.4 = ((bf16[16,16,1792]{2,1,0:T(8,128)(2,1)}), bf16[16,16,1792]{2,1,0:T(8,128)(2,1)S(1)}, u32[]{:S(2)}, u32[]{:S(2)}) async-start(bf16[16,16,1792]{2,1,0:T(8,128)(2,1)} %stack.2), calls=%async_computation.4 | async-start | bytes 1835008 | tf_op jit(solution)/shard_map/all_to_all | solution.py:17
Sparse Core Ops, SparseCore 0:
  10.4 67.8 all-gather.2
